TPU v7x, 128 devices: a whole 4x4x4 slice. The times are simulated.
128 devices in a mesh: blk: 64 (over z, x_hi, y, core), feat: 2 (over x_lo).
Axes of the slice: x: 4 (x_hi: 2, x_lo: 2; x = x_hi * 2 + x_lo), y: 4, z: 4, core: 2. Of those that a mesh axis runs over, the one named last changes fastest.
Arguments:
- embeddings: float32 [32768, 2048], P('blk', 'feat')
- partner: int32 [32768], P('blk'), may hold values from 0 to 32767, as said below
Outputs:
- loss: float32 [], replicated
- grads: float32 [32768, 2048], P('blk', 'feat')
Inputs may be any that keep to these rules, and one draw needn't show every extreme that they name: `partner`: partner_i is never i and lies in a block at cycle distance at most 4 from the block of row i (blocks of 512 consecutive rows, block 63 next to block 0).
All inputs are finite; a program needn't handle non-finite values.
Results may differ from a plain program's by a relative error of at most 0.0003.
Values sent between devices are 32-bit elements; how exact they have to be, the bound alone decides.
No kernel may reach another device: no remote copies, remote signals or barrier semaphores. Data moves between devices by JAX's collectives and lax.ppermute only.
A program may use at most 128 MiB of HBM per device.

v0:
```python
import jax
import jax.numpy as jnp
from jax import lax
from jax.sharding import PartitionSpec as P

REACH = 4


sharpness_divisor = 0.1
score_shift = 10.0


def shifted(value, axis, steps):
    count = lax.axis_size(axis)
    pairs = [(source, (source + steps) % count) for source in range(count)]
    return lax.ppermute(value, axis, pairs)


def pairwise_cosine_matrix(left, right):
    return lax.dot_general(
        left,
        right,
        (((1,), (1,)), ((), ())),
        precision=lax.Precision.HIGHEST,
        preferred_element_type=jnp.float32,
    )


def sharpened_right_similarities(left, right):
    return jnp.dot(left, right, precision=lax.Precision.HIGHEST, preferred_element_type=jnp.float32)


def block_ids(here_block, offset, block_count, within, rows_count):
    return (here_block + offset) % block_count * rows_count + within


def band_values(values, offsets):
    stacked = []
    for offset in offsets:
        if offset == 0:
            stacked.append(values)
        else:
            stacked.append(shifted(values, "blk", -offset))
    return jnp.stack(stacked, axis=0)


def coefficients(
    similarity_energies,
    kept,
    lse_rows,
    lse_cols,
    count_rows,
    count_cols,
    part_rows,
    part_cols,
    row_ids,
    col_ids,
):
    probs = jnp.where(kept, jnp.exp(similarity_energies - lse_rows[:, None]), 0.0)
    probs_back = jnp.where(kept, jnp.exp(similarity_energies - lse_cols[None, :]), 0.0)
    hits = (col_ids[None, :] == part_rows[:, None]).astype(jnp.float32)
    hits_back = (part_cols[None, :] == row_ids[:, None]).astype(jnp.float32)
    return (count_rows[:, None] * probs + count_cols[None, :] * probs_back) * 0.5 - hits - hits_back


def per_device(embeddings, partner):
    rows_count = embeddings.shape[0]
    here_block = lax.axis_index("blk")
    block_count = lax.axis_size("blk")
    within = jnp.arange(rows_count, dtype=jnp.int32)
    row_ids = here_block * rows_count + within
    squares = lax.psum(jnp.sum(embeddings * embeddings, axis=1), "feat")
    norms = jnp.sqrt(squares + 1e-06)
    left_unit_embeddings = embeddings / norms[:, None]
    table = lax.all_gather(partner, "blk", axis=0, tiled=True)
    total_rows = table.shape[0]
    counts_all = 1.0 + jax.ops.segment_sum(
        jnp.ones((total_rows,), jnp.float32), table, num_segments=total_rows
    )
    count_rows = counts_all[row_ids]
    pieces = []
    id_list = []
    for offset in range(-REACH, REACH + 1):
        if offset == 0:
            pieces.append(left_unit_embeddings)
        else:
            pieces.append(shifted(left_unit_embeddings, "blk", -offset))
        id_list.append(block_ids(here_block, offset, block_count, within, rows_count))
    embedding_matrix_right = jnp.concatenate(pieces, axis=0)
    col_ids = jnp.concatenate(id_list, axis=0)
    part_cols = table[col_ids]
    similarity_energies = (
        lax.psum(pairwise_cosine_matrix(left_unit_embeddings, embedding_matrix_right), "feat")
        / sharpness_divisor
    )
    kept = col_ids[None, :] != row_ids[:, None]
    expo = jnp.where(kept, jnp.exp(similarity_energies - score_shift), 0.0)
    lse = score_shift + jnp.log(jnp.sum(expo, axis=1))
    spos = jnp.sum(
        jnp.where(col_ids[None, :] == partner[:, None], similarity_energies, 0.0), axis=1
    )
    lse_cols = band_values(lse, range(-REACH, REACH + 1)).reshape(-1)
    mixing_coefficient_matrix = coefficients(
        similarity_energies,
        kept,
        lse,
        lse_cols,
        count_rows,
        counts_all[col_ids],
        partner,
        part_cols,
        row_ids,
        col_ids,
    )
    derivative_wrt_unit_embeddings = (
        sharpened_right_similarities(mixing_coefficient_matrix, embedding_matrix_right)
        / sharpness_divisor
    )
    loss_local = jnp.sum(count_rows * lse * 0.5 - spos)
    loss = lax.psum(loss_local, "blk") / total_rows
    proj = lax.psum(jnp.sum(left_unit_embeddings * derivative_wrt_unit_embeddings, axis=1), "feat")
    grads = (derivative_wrt_unit_embeddings - left_unit_embeddings * proj[:, None]) / norms[:, None]
    return (loss, grads)


def solution(mesh):
    in_specs = (P("blk", "feat"), P("blk"))
    out_specs = (P(), P("blk", "feat"))
    return jax.shard_map(
        per_device, mesh=mesh, in_specs=in_specs, out_specs=out_specs, check_vma=False
    )
```

profile of v0, /device:TPU:0, one launch (start us, length us, event | category | flops | bytes accessed | tf_op | source)
XLA Modules:
  0.0 894.4 jit_solution(16707813413321090903)
XLA Ops:
  7.2 0.0 all-reduce.2.cloned.1.call-start
  7.2 1.8 multiply_reduce_fusion.1
  9.0 4.9 psum.28
  14.0 1.8 broadcast_divide_fusion
  15.8 3.3 collective-permute-start
  19.2 0.8 collective-permute-start.2
  19.9 3.4 collective-permute-start.3
  23.4 5.8 collective-permute-start.4
  29.2 42.7 %collective-permute-done = f32[512,1024]{1,0:T(8,128)S(1)} collective-permute-done((f32[512,1024]{1,0:T(8,128)S(1)}, f32[512,1024]{1,0:T(8,128)S(1)}, u32[]{:S(2)}, u32[]{:S(2)}) %collective-permute-start) | collective-permute-done | bytes 2097184 | tf_op jit(solution)/shard_map/ppermute | solution.py:16
  71.9 25.6 %collective-permute-start.5 = (f32[512,1024]{1,0:T(8,128)S(1)}, f32[512,1024]{1,0:T(8,128)S(1)}, u32[]{:S(2)}, u32[]{:S(2)}) collective-permute-start(f32[512,1024]{1,0:T(8,128)S(1)} %broadcast_divide_fusion), channel_id=1, source_target_pairs={{0,124},{2,126},{4,0},{6,2},{8,4},{10,6},{12,8},{14,10},{16,12},{1... | collective-permute-start | bytes 6291464 | tf_op jit(solution)/shard_map/ppermute | solution.py:16
  97.5 12.8 %collective-permute-done.1 = f32[512,1024]{1,0:T(8,128)S(1)} collective-permute-done((f32[512,1024]{1,0:T(8,128)S(1)}, f32[512,1024]{1,0:T(8,128)S(1)}, u32[]{:S(2)}, u32[]{:S(2)}) %collective-permute-start.1) | collective-permute-done | bytes 2097184 | tf_op jit(solution)/shard_map/ppermute | solution.py:16
  110.3 29.7 %collective-permute-start.6 = (f32[512,1024]{1,0:T(8,128)S(1)}, f32[512,1024]{1,0:T(8,128)S(1)}, u32[]{:S(2)}, u32[]{:S(2)}) collective-permute-start(f32[512,1024]{1,0:T(8,128)S(1)} %broadcast_divide_fusion), channel_id=1, source_target_pairs={{0,122},{2,124},{4,126},{6,0},{8,2},{10,4},{12,6},{14,8},{16,10},{... | collective-permute-start | bytes 6291464 | tf_op jit(solution)/shard_map/ppermute | solution.py:16
  139.9 22.4 %collective-permute-done.2 = f32[512,1024]{1,0:T(8,128)S(1)} collective-permute-done((f32[512,1024]{1,0:T(8,128)S(1)}, f32[512,1024]{1,0:T(8,128)S(1)}, u32[]{:S(2)}, u32[]{:S(2)}) %collective-permute-start.2) | collective-permute-done | bytes 2097184 | tf_op jit(solution)/shard_map/ppermute | solution.py:16
  162.3 22.8 %collective-permute-start.7 = (f32[512,1024]{1,0:T(8,128)S(1)}, f32[512,1024]{1,0:T(8,128)S(1)}, u32[]{:S(2)}, u32[]{:S(2)}) collective-permute-start(f32[512,1024]{1,0:T(8,128)S(1)} %broadcast_divide_fusion), channel_id=1, source_target_pairs={{0,120},{2,122},{4,124},{6,126},{8,0},{10,2},{12,4},{14,6},{16,8},... | collective-permute-start | bytes 6291464 | tf_op jit(solution)/shard_map/ppermute | solution.py:16
  185.1 0.1 constant_dynamic-update-slice_fusion.9
  185.3 0.1 constant_dynamic-update-slice_fusion.8
  185.4 0.1 constant_dynamic-update-slice_fusion.7
  185.6 0.1 constant_dynamic-update-slice_fusion.6
  185.7 0.2 constant_dynamic-update-slice_fusion.5
  186.0 0.1 constant_dynamic-update-slice_fusion.4
  186.2 85.8 %collective-permute-done.5 = f32[512,1024]{1,0:T(8,128)S(1)} collective-permute-done((f32[512,1024]{1,0:T(8,128)S(1)}, f32[512,1024]{1,0:T(8,128)S(1)}, u32[]{:S(2)}, u32[]{:S(2)}) %collective-permute-start.5) | collective-permute-done | bytes 2097184 | tf_op jit(solution)/shard_map/ppermute | solution.py:16
  272.0 0.1 constant_dynamic-update-slice_fusion.3
  272.1 20.0 %collective-permute-done.6 = f32[512,1024]{1,0:T(8,128)S(1)} collective-permute-done((f32[512,1024]{1,0:T(8,128)S(1)}, f32[512,1024]{1,0:T(8,128)S(1)}, u32[]{:S(2)}, u32[]{:S(2)}) %collective-permute-start.6) | collective-permute-done | bytes 2097184 | tf_op jit(solution)/shard_map/ppermute | solution.py:16
  292.1 0.1 constant_dynamic-update-slice_fusion.2
  292.3 0.1 constant_dynamic-update-slice_fusion.1
  292.4 6.5 copy-done.1
  298.9 32.3 %fusion.34 = f32[512,4608]{1,0:T(8,128)} fusion(f32[512,1024]{1,0:T(8,128)S(1)} %broadcast_divide_fusion, f32[4608,1024]{1,0:T(8,128)S(1)} %constant_dynamic-update-slice_fusion.1), kind=kOutput, calls=%fused_computation.88 | convolution fusion | flops 28991029248 | bytes 30408704 | tf_op jit(solution)/shard_map/dot_general | solution.py:20
  331.4 0.5 copy-done.3
  331.9 88.6 %all-gather = s32[64,1,512]{2,1,0:T(1,128)S(1)} all-gather(s32[1,1,512]{2,1,0:T(1,128)S(1)} %bitcast.26), channel_id=1, replica_groups=mesh['blk'=64,'feat'=2] {'blk'}, dimensions={0}, use_global_device_ids=true | all-gather | bytes 133120 | tf_op jit(solution)/shard_map/all_gather | solution.py:75
  420.5 175.1 %scatter_fusion = f32[32768]{0:T(1024)S(1)} fusion(f32[32768]{0:T(1024)S(1)} %broadcast_in_dim.11, s32[32768]{0:T(1024)S(1)} %bitcast.24, f32[32768]{0:T(1024)S(1)} %broadcast_in_dim.11), kind=kCustom, calls=%fused_computation.3 | custom fusion | flops 32768 | bytes 524288 | tf_op jit(solution)/shard_map/scatter-add | solution.py:77
  595.7 3.1 gather_fusion
  599.2 6.3 fusion.5
  605.5 0.6 log_add_fusion
  606.1 1.9 collective-permute-start.9
  608.0 0.1 collective-permute-start.10
  608.1 0.1 fusion.30
  608.1 0.2 collective-permute-start.11
  608.3 7.4 collective-permute-start.12
  615.7 1.9 collective-permute-start.13
  617.7 0.8 collective-permute-start.14
  618.5 4.7 collective-permute-start.15
  623.1 24.1 %gather_fusion.2 = s32[4608]{0:T(1024)S(1)} fusion(s32[32768]{0:T(1024)S(1)} %bitcast.25, s32[5120]{0:T(1024)S(1)} %pad_clamp_fusion), kind=kCustom, calls=%fused_computation.2 | custom fusion | bytes 55296 | tf_op jit(solution)/shard_map/gather | solution.py:91
  647.2 24.1 %gather_fusion.1 = f32[4608]{0:T(1024)S(1)} fusion(f32[32768]{0:T(1024)S(1)} %scatter_fusion, s32[5120]{0:T(1024)S(1)} %pad_clamp_fusion), kind=kCustom, calls=%fused_computation.1 | custom fusion | bytes 55296 | tf_op jit(solution)/shard_map/gather | solution.py:109
  671.3 163.9 %psum.30 = f32[]{:T(128)} all-reduce(f32[]{:T(128)} %get-tuple-element.5), channel_id=1, replica_groups=mesh['blk'=64,'feat'=2] {'blk'}, use_global_device_ids=true, to_apply=%region_7.8 | all-reduce | flops 1 | bytes 8 | tf_op jit(solution)/shard_map/psum | solution.py:120
  835.9 0.1 stack.36
  836.0 42.2 %multiply_reduce_fusion = (f32[512]{0:T(512)S(1)}, f32[512,1024]{1,0:T(8,128)}) fusion(f32[512,1024]{1,0:T(8,128)} %copy-done.2, f32[4608,1024]{1,0:T(8,128)} %copy-done.1, f32[512,4608]{1,0:T(8,128)} %all-reduce.2.cloned.1.call-done, s32[4608]{0:T(1024)S(1)} %gather_fusion.2, f32[4608]{0:T(1024)S(1)} %sub.38, f32[4608]{0:T(1024)S(1)} %gather_fusion.1, ...), kind=kOutput, calls=%fused_computation.37 | convolution fusion | flops 29030350848 | bytes 32589824 | tf_op jit(solution)/shard_map/dot_general | solution.py:30
  878.1 4.9 psum.31
  883.1 3.3 subtract_divide_fusion
  (55 shorter events, 0.4 us)
Async XLA Ops:
  7.2 592.0 %all-reduce.2.cloned.1.call-start = ((), (), s32[]{:S(2)}) async-start(), calls=%async_computation | async-start | bytes 18874368 | tf_op jit(solution)/shard_map/psum | solution.py:93
  15.8 276.6 %copy-start.2 = (f32[512,1024]{1,0:T(8,128)}, f32[512,1024]{1,0:T(8,128)S(1)}, u32[]{:S(2)}) copy-start(f32[512,1024]{1,0:T(8,128)S(1)} %broadcast_divide_fusion) | copy-start | bytes 6291460
  15.8 169.9 %copy-start = (f32[512,1024]{1,0:T(8,128)S(1)}, f32[512,1024]{1,0:T(8,128)}, u32[]{:S(2)}) copy-start(f32[512,1024]{1,0:T(8,128)} %param.2) | copy-start | bytes 6291460
  15.8 56.0 %collective-permute-start = (f32[512,1024]{1,0:T(8,128)S(1)}, f32[512,1024]{1,0:T(8,128)S(1)}, u32[]{:S(2)}, u32[]{:S(2)}) collective-permute-start(f32[512,1024]{1,0:T(8,128)S(1)} %broadcast_divide_fusion), channel_id=1, source_target_pairs={{0,8},{2,10},{4,12},{6,14},{8,16},{10,18},{12,20},{14,22},{16,24},... | collective-permute-start | bytes 6291464 | tf_op jit(solution)/shard_map/ppermute | solution.py:16
  19.2 91.1 %collective-permute-start.1 = (f32[512,1024]{1,0:T(8,128)S(1)}, f32[512,1024]{1,0:T(8,128)S(1)}, u32[]{:S(2)}, u32[]{:S(2)}) collective-permute-start(f32[512,1024]{1,0:T(8,128)S(1)} %broadcast_divide_fusion), channel_id=1, source_target_pairs={{0,6},{2,8},{4,10},{6,12},{8,14},{10,16},{12,18},{14,20},{16,22},{... | collective-permute-start | bytes 6291464 | tf_op jit(solution)/shard_map/ppermute | solution.py:16
  19.2 143.1 %collective-permute-start.2 = (f32[512,1024]{1,0:T(8,128)S(1)}, f32[512,1024]{1,0:T(8,128)S(1)}, u32[]{:S(2)}, u32[]{:S(2)}) collective-permute-start(f32[512,1024]{1,0:T(8,128)S(1)} %broadcast_divide_fusion), channel_id=1, source_target_pairs={{0,4},{2,6},{4,8},{6,10},{8,12},{10,14},{12,16},{14,18},{16,20},{1... | collective-permute-start | bytes 6291464 | tf_op jit(solution)/shard_map/ppermute | solution.py:16
  19.9 165.6 %collective-permute-start.3 = (f32[512,1024]{1,0:T(8,128)S(1)}, f32[512,1024]{1,0:T(8,128)S(1)}, u32[]{:S(2)}, u32[]{:S(2)}) collective-permute-start(f32[512,1024]{1,0:T(8,128)S(1)} %broadcast_divide_fusion), channel_id=1, source_target_pairs={{0,2},{2,4},{4,6},{6,8},{8,10},{10,12},{12,14},{14,16},{16,18},{18... | collective-permute-start | bytes 6291464 | tf_op jit(solution)/shard_map/ppermute | solution.py:16
  23.4 162.6 %collective-permute-start.4 = (f32[512,1024]{1,0:T(8,128)S(1)}, f32[512,1024]{1,0:T(8,128)S(1)}, u32[]{:S(2)}, u32[]{:S(2)}) collective-permute-start(f32[512,1024]{1,0:T(8,128)S(1)} %broadcast_divide_fusion), channel_id=1, source_target_pairs={{0,126},{2,0},{4,2},{6,4},{8,6},{10,8},{12,10},{14,12},{16,14},{18... | collective-permute-start | bytes 6291464 | tf_op jit(solution)/shard_map/ppermute | solution.py:16
  71.9 200.1 %collective-permute-start.5 = (f32[512,1024]{1,0:T(8,128)S(1)}, f32[512,1024]{1,0:T(8,128)S(1)}, u32[]{:S(2)}, u32[]{:S(2)}) collective-permute-start(f32[512,1024]{1,0:T(8,128)S(1)} %broadcast_divide_fusion), channel_id=1, source_target_pairs={{0,124},{2,126},{4,0},{6,2},{8,4},{10,6},{12,8},{14,10},{16,12},{1... | collective-permute-start | bytes 6291464 | tf_op jit(solution)/shard_map/ppermute | solution.py:16
  110.3 181.9 %collective-permute-start.6 = (f32[512,1024]{1,0:T(8,128)S(1)}, f32[512,1024]{1,0:T(8,128)S(1)}, u32[]{:S(2)}, u32[]{:S(2)}) collective-permute-start(f32[512,1024]{1,0:T(8,128)S(1)} %broadcast_divide_fusion), channel_id=1, source_target_pairs={{0,122},{2,124},{4,126},{6,0},{8,2},{10,4},{12,6},{14,8},{16,10},{... | collective-permute-start | bytes 6291464 | tf_op jit(solution)/shard_map/ppermute | solution.py:16
  162.3 129.9 %collective-permute-start.7 = (f32[512,1024]{1,0:T(8,128)S(1)}, f32[512,1024]{1,0:T(8,128)S(1)}, u32[]{:S(2)}, u32[]{:S(2)}) collective-permute-start(f32[512,1024]{1,0:T(8,128)S(1)} %broadcast_divide_fusion), channel_id=1, source_target_pairs={{0,120},{2,122},{4,124},{6,126},{8,0},{10,2},{12,4},{14,6},{16,8},... | collective-permute-start | bytes 6291464 | tf_op jit(solution)/shard_map/ppermute | solution.py:16
  292.4 6.5 copy-start.1
  331.2 0.7 copy-start.3
  606.1 9.6 %collective-permute-start.8 = (f32[512]{0:T(512)S(1)}, f32[512]{0:T(512)S(1)}, u32[]{:S(2)}, u32[]{:S(2)}) collective-permute-start(f32[512]{0:T(512)S(1)} %get-tuple-element.4), channel_id=1, source_target_pairs={{0,8},{2,10},{4,12},{6,14},{8,16},{10,18},{12,20},{14,22},{16,24},... | collective-permute-start | bytes 6152 | tf_op jit(solution)/shard_map/ppermute | solution.py:16
  606.1 11.6 %collective-permute-start.9 = (f32[512]{0:T(512)S(1)}, f32[512]{0:T(512)S(1)}, u32[]{:S(2)}, u32[]{:S(2)}) collective-permute-start(f32[512]{0:T(512)S(1)} %get-tuple-element.4), channel_id=1, source_target_pairs={{0,6},{2,8},{4,10},{6,12},{8,14},{10,16},{12,18},{14,20},{16,22},{... | collective-permute-start | bytes 6152 | tf_op jit(solution)/shard_map/ppermute | solution.py:16
  608.0 10.5 %collective-permute-start.10 = (f32[512]{0:T(512)S(1)}, f32[512]{0:T(512)S(1)}, u32[]{:S(2)}, u32[]{:S(2)}) collective-permute-start(f32[512]{0:T(512)S(1)} %get-tuple-element.4), channel_id=1, source_target_pairs={{0,4},{2,6},{4,8},{6,10},{8,12},{10,14},{12,16},{14,18},{16,20},{1... | collective-permute-start | bytes 6152 | tf_op jit(solution)/shard_map/ppermute | solution.py:16
  608.1 227.7 %collective-permute-start.11 = (f32[512]{0:T(512)S(1)}, f32[512]{0:T(512)S(1)}, u32[]{:S(2)}, u32[]{:S(2)}) collective-permute-start(f32[512]{0:T(512)S(1)} %get-tuple-element.4), channel_id=1, source_target_pairs={{0,2},{2,4},{4,6},{6,8},{8,10},{10,12},{12,14},{14,16},{16,18},{18... | collective-permute-start | bytes 6152 | tf_op jit(solution)/shard_map/ppermute | solution.py:16
  608.3 227.6 %collective-permute-start.12 = (f32[512]{0:T(512)S(1)}, f32[512]{0:T(512)S(1)}, u32[]{:S(2)}, u32[]{:S(2)}) collective-permute-start(f32[512]{0:T(512)S(1)} %get-tuple-element.4), channel_id=1, source_target_pairs={{0,126},{2,0},{4,2},{6,4},{8,6},{10,8},{12,10},{14,12},{16,14},{18... | collective-permute-start | bytes 6152 | tf_op jit(solution)/shard_map/ppermute | solution.py:16
  615.7 220.2 %collective-permute-start.13 = (f32[512]{0:T(512)S(1)}, f32[512]{0:T(512)S(1)}, u32[]{:S(2)}, u32[]{:S(2)}) collective-permute-start(f32[512]{0:T(512)S(1)} %get-tuple-element.4), channel_id=1, source_target_pairs={{0,124},{2,126},{4,0},{6,2},{8,4},{10,6},{12,8},{14,10},{16,12},{1... | collective-permute-start | bytes 6152 | tf_op jit(solution)/shard_map/ppermute | solution.py:16
  617.7 218.3 %collective-permute-start.14 = (f32[512]{0:T(512)S(1)}, f32[512]{0:T(512)S(1)}, u32[]{:S(2)}, u32[]{:S(2)}) collective-permute-start(f32[512]{0:T(512)S(1)} %get-tuple-element.4), channel_id=1, source_target_pairs={{0,122},{2,124},{4,126},{6,0},{8,2},{10,4},{12,6},{14,8},{16,10},{... | collective-permute-start | bytes 6152 | tf_op jit(solution)/shard_map/ppermute | solution.py:16
  618.5 217.4 %collective-permute-start.15 = (f32[512]{0:T(512)S(1)}, f32[512]{0:T(512)S(1)}, u32[]{:S(2)}, u32[]{:S(2)}) collective-permute-start(f32[512]{0:T(512)S(1)} %get-tuple-element.4), channel_id=1, source_target_pairs={{0,120},{2,122},{4,124},{6,126},{8,0},{10,2},{12,4},{14,6},{16,8},... | collective-permute-start | bytes 6152 | tf_op jit(solution)/shard_map/ppermute | solution.py:16
Sparse Core Ops, SparseCore 0:
  331.4 250.6 all-reduce.1
where the time goes:
time: 895 us; the launch traced here: 894 us
  blocking collectives  262 us (29%)
  other arithmetic  189 us (21%)
  waiting for transfers between devices  184 us (21%)
  starting transfers between devices  108 us (12%)
  matrix products  74.5 us (8%)
  local copies, waits for them, and re-layouts  59.5 us (7%)
  between operations  16.4 us (2%)
    ppermute x16, waiting for transfers between devices, shifted(): return lax.ppermute(value, axis, pairs)  184 us
    scatter-add x1, other arithmetic, per_device(): jax.ops.segment_sum(jnp.ones((total_rows,), jnp.float32), table, num_segm...  175 us
    psum x1, blocking collectives, per_device(): loss = lax.psum(loss_local, 'blk') / total_rows  164 us
    ppermute x16, starting transfers between devices, shifted(): return lax.ppermute(value, axis, pairs)  108 us
    all_gather x1, blocking collectives, per_device(): table = lax.all_gather(partner, 'blk', axis=0, tiled=True)  88.6 us
    dot_general x1, matrix products, sharpened_right_similarities(): jnp.dot(left, right, precision=lax.Precision.HIGHEST, preferred_element_t...  42.2 us
    dot_general x1, matrix products, pairwise_cosine_matrix(): lax.dot_general(left, right, (((1,), (1,)), ((), ())), precision=lax.Prec...  32.3 us
    gather x1, local copies, waits for them, and re-layouts, per_device(): counts_all[col_ids]  24.1 us
  transfers between devices with their start and end apart: 17, of which 5 were waited for; matrix products, arithmetic and copies ran while one was open for 25% of the time, Pallas kernels for 0%

commit v1 on v0

v1 whole, which is shorter than its diff:
```python
import functools

import jax
import jax.numpy as jnp
from jax import lax
from jax.experimental import pallas as pl
from jax.experimental.pallas import tpu as pltpu
from jax.sharding import PartitionSpec as P

R = 512
F = 1024
F32 = jnp.float32
BF16 = jnp.bfloat16
VMEM = 56 * 1024 * 1024
NT = (((1,), (1,)), ((), ()))
NN = (((1,), (0,)), ((), ()))
M, E, O, X, N = range(5)
LEFT = ((M, E, O, X, O), (M, X, O, X, O))
RIGHT = ((N, N, N, N, O), (N, N, N, O, O))


def split(v):
    hi = v.astype(BF16)
    return hi, (v - hi.astype(F32)).astype(BF16)


def dot3(ah, al, bh, bl, dims):
    def one(a, b):
        return lax.dot_general(a, b, dims, preferred_element_type=F32)

    return one(ah, bh) + one(ah, bl) + one(al, bh)


def pick(par, table, s):
    even = jnp.int32(table[0][0])
    odd = jnp.int32(table[1][0])
    for k in range(1, len(table[0])):
        even = jnp.where(s == k, table[0][k], even)
        odd = jnp.where(s == k, table[1][k], odd)
    return jnp.where(par == 0, even, odd)


def scores_kernel(lefts, par_ref, *refs):
    names = sorted(set(lefts[0]) | set(lefts[1]))
    ins = dict(zip(names, refs[: len(names)]))
    right, out = refs[len(names)], refs[len(names) + 1]
    lbuf, rbuf, rh, rl, ob, lsem, rsem, osem = refs[len(names) + 2 :]
    par = par_ref[0]
    pltpu.make_async_copy(right, rbuf, rsem).start()
    for p in (0, 1):

        @pl.when(par == p)
        def _():
            for s, name in enumerate(lefts[p]):
                pltpu.make_async_copy(ins[name], lbuf.at[s], lsem.at[s]).start()

    pltpu.make_async_copy(right, rbuf, rsem).wait()
    hi, lo = split(rbuf[...])
    rh[...] = hi
    rl[...] = lo
    count = jnp.where(par == 0, len(lefts[0]), len(lefts[1]))

    def step(s, _):
        pltpu.make_async_copy(right, lbuf.at[s], lsem.at[s]).wait()

        def rows(k, _):
            at = pl.ds(pl.multiple_of(k * 128, 128), 128)
            lh, ll = split(lbuf[s, at, :])
            ob[s, at, :] = dot3(lh, ll, rh[...], rl[...], NT)
            return 0

        lax.fori_loop(0, R // 128, rows, 0)
        pltpu.make_async_copy(ob.at[s], out.at[s], osem.at[s]).start()
        return 0

    lax.fori_loop(0, count, step, 0)

    def drain(s, _):
        pltpu.make_async_copy(ob.at[s], out.at[s], osem.at[s]).wait()
        return 0

    lax.fori_loop(0, count, drain, 0)


def partial_scores(par, blocks, right, lefts):
    slots = max(len(lefts[0]), len(lefts[1]))
    names = sorted(set(lefts[0]) | set(lefts[1]))
    return pl.pallas_call(
        functools.partial(scores_kernel, lefts),
        out_shape=jax.ShapeDtypeStruct((slots, R, R), F32),
        in_specs=[pl.BlockSpec(memory_space=pltpu.SMEM)] + [pl.BlockSpec(memory_space=pl.ANY)] * (len(names) + 1),
        out_specs=pl.BlockSpec(memory_space=pl.ANY),
        scratch_shapes=[
            pltpu.VMEM((slots, R, F), F32),
            pltpu.VMEM((R, F), F32),
            pltpu.VMEM((R, F), BF16),
            pltpu.VMEM((R, F), BF16),
            pltpu.VMEM((slots, R, R), F32),
            pltpu.SemaphoreType.DMA((slots,)),
            pltpu.SemaphoreType.DMA,
            pltpu.SemaphoreType.DMA((slots,)),
        ],
        compiler_params=pltpu.CompilerParams(vmem_limit_bytes=VMEM),
        cost_estimate=pl.CostEstimate(flops=slots * 6 * R * R * F, bytes_accessed=(slots + 1) * R * F * 4, transcendentals=0),
        name="partial_scores",
    )(par, *[blocks[k] for k in names], right)


def columns(rows):
    return jnp.transpose(rows)


def sums_kernel(par_ref, mine, theirs, vec, s_out, t_out):
    s = pl.program_id(0)
    par = par_ref[0]
    left, right = pick(par, LEFT, s), pick(par, RIGHT, s)

    @pl.when(s == 0)
    def _():
        t_out[...] = jnp.zeros_like(t_out)

    inv_j = vec[right, 0:1, :]
    inv_i = columns(vec[left])[:, 0:1] * 10.0
    diag = s == 4
    for k in range(R // 128):
        at = slice(k * 128, (k + 1) * 128)
        sc = (mine[0, at, :] + theirs[0, at, :]) * (inv_i[at] * inv_j)
        s_out[0, at, :] = sc
        ex = jnp.exp(sc - 10.0)
        r = lax.broadcasted_iota(jnp.int32, (128, R), 0) + k * 128
        c = lax.broadcasted_iota(jnp.int32, (128, R), 1)
        ex = jnp.where(jnp.logical_and(diag, r == c), 0.0, ex)
        lanes = ex[:, 0:128] + ex[:, 128:256] + ex[:, 256:384] + ex[:, 384:512]
        t_out[left, 0:1, at] += jnp.sum(jnp.transpose(lanes), axis=0, keepdims=True)
        down = jnp.sum(ex, axis=0, keepdims=True)
        t_out[right, 0:1, :] += jnp.where(diag, 0.0, down)


def score_sums(par, mine, theirs, vec):
    one = lambda s: (s, 0, 0)
    whole = lambda s: (0, 0, 0)
    return pl.pallas_call(
        sums_kernel,
        grid=(5,),
        out_shape=(jax.ShapeDtypeStruct((5, R, R), F32), jax.ShapeDtypeStruct((5, 8, R), F32)),
        in_specs=[
            pl.BlockSpec(memory_space=pltpu.SMEM),
            pl.BlockSpec((1, R, R), one),
            pl.BlockSpec((1, R, R), one),
            pl.BlockSpec((5, 8, R), whole),
        ],
        out_specs=(pl.BlockSpec((1, R, R), one), pl.BlockSpec((5, 8, R), whole)),
        compiler_params=pltpu.CompilerParams(vmem_limit_bytes=VMEM),
        name="score_sums",
    )(par, mine, theirs, vec)


def coef_kernel(par_ref, sc_ref, vec, ids, ch, cl, th, tl, t_out, spos_out):
    s = pl.program_id(0)
    par = par_ref[0]
    left, right = pick(par, LEFT, s), pick(par, RIGHT, s)

    @pl.when(s == 0)
    def _():
        t_out[...] = jnp.zeros_like(t_out)
        spos_out[...] = jnp.zeros_like(spos_out)

    cols = columns(vec[left])
    part_i = cols[:, 1:2].astype(jnp.int32) - ids[right]
    a_i = cols[:, 2:3]
    part_j = vec[right, 1:2, :].astype(jnp.int32) - ids[left]
    a_j = vec[right, 2:3, :]
    diag = s == 4
    for k in range(R // 128):
        at = slice(k * 128, (k + 1) * 128)
        sc = sc_ref[0, at, :]
        r = lax.broadcasted_iota(jnp.int32, (128, R), 0) + k * 128
        c = lax.broadcasted_iota(jnp.int32, (128, R), 1)
        ex = jnp.where(jnp.logical_and(diag, r == c), 0.0, jnp.exp(sc - 10.0))
        hits = (part_i[at] == c).astype(F32)
        back = (part_j == r).astype(F32)
        cf = ex * (a_i[at] + a_j) - hits - back
        hs = sc * (hits + jnp.where(diag, 0.0, back))
        spos_out[...] += jnp.sum(hs.reshape(16, 8, R), axis=0)
        pr = cf * sc
        lanes = pr[:, 0:128] + pr[:, 128:256] + pr[:, 256:384] + pr[:, 384:512]
        t_out[left, 0:1, at] += jnp.sum(jnp.transpose(lanes), axis=0, keepdims=True)
        down = jnp.sum(pr, axis=0, keepdims=True)
        t_out[right, 0:1, :] += jnp.where(diag, 0.0, down)
        hi, lo = split(cf)
        ch[0, at, :] = hi
        cl[0, at, :] = lo
        hi, lo = split(jnp.transpose(cf))
        th[0, :, at] = hi
        tl[0, :, at] = lo


def coefficients(par, scores, vec, ids):
    one = lambda s: (s, 0, 0)
    whole = lambda s: (0, 0, 0)
    mat = pl.BlockSpec((1, R, R), one)
    half = jax.ShapeDtypeStruct((5, R, R), BF16)
    return pl.pallas_call(
        coef_kernel,
        grid=(5,),
        out_shape=(half, half, half, half, jax.ShapeDtypeStruct((5, 8, R), F32), jax.ShapeDtypeStruct((8, R), F32)),
        in_specs=[
            pl.BlockSpec(memory_space=pltpu.SMEM),
            mat,
            pl.BlockSpec((5, 8, R), whole),
            pl.BlockSpec(memory_space=pltpu.SMEM),
        ],
        out_specs=(mat, mat, mat, mat, pl.BlockSpec((5, 8, R), whole), pl.BlockSpec((8, R), lambda s: (0, 0))),
        compiler_params=pltpu.CompilerParams(vmem_limit_bytes=VMEM),
        name="coefficients",
    )(par, scores, vec, ids)


def units_kernel(m, e, o, x, n, vec, uh, ul):
    k = pl.program_id(0)
    for j, ref in enumerate((m, e, o, x, n)):
        inv = columns(vec[j])[:, 0:1]
        hi, lo = split(ref[...] * inv)
        uh[j] = hi
        ul[j] = lo


def split_units(blocks, vec):
    cell = pl.BlockSpec((R, 256), lambda k: (0, k))
    res = pl.BlockSpec((5, R, 256), lambda k: (0, 0, k))
    shape = jax.ShapeDtypeStruct((5, R, F), BF16)
    return pl.pallas_call(
        units_kernel,
        grid=(F // 256,),
        out_shape=(shape, shape),
        in_specs=[cell] * 5 + [pl.BlockSpec((5, 8, R), lambda k: (0, 0, 0))],
        out_specs=(res, res),
        compiler_params=pltpu.CompilerParams(vmem_limit_bytes=VMEM),
        name="split_units",
    )(*blocks, vec)


def contrib_kernel(plans, par_ref, ch, cl, th, tl, uh, ul, proj, *refs):
    outs = refs
    par = par_ref[0]
    f = pl.program_id(0)
    for p in (0, 1):

        @pl.when(par == p)
        def _():
            for (name, terms), out in zip(plans[p], outs):
                total = None
                for transposed, s, u in terms:
                    a = (th, tl) if transposed else (ch, cl)
                    t = dot3(a[0][s], a[1][s], uh[u], ul[u], NN)
                    total = t if total is None else total + t
                if total is not None:
                    out[0:R, :] = total
                else:
                    out[0:R, :] = jnp.zeros((R, out.shape[1]), F32)
                out[R : R + 8, 0:R] = proj[name]


def contributions(par, mats, units, proj, plans):
    T = 512
    whole = pl.BlockSpec((5, R, R), lambda f: (0, 0, 0))
    cell = pl.BlockSpec((5, R, T), lambda f: (0, 0, f))
    count = len(plans[0])
    terms = sum(len(t) for _, t in plans[0])
    return pl.pallas_call(
        functools.partial(contrib_kernel, plans),
        grid=(F // T,),
        out_shape=[jax.ShapeDtypeStruct((R + 8, F), F32)] * count,
        in_specs=[pl.BlockSpec(memory_space=pltpu.SMEM)] + [whole] * 4 + [cell] * 2 + [pl.BlockSpec((5, 8, R), lambda f: (0, 0, 0))],
        out_specs=[pl.BlockSpec((R + 8, T), lambda f: (0, f))] * count,
        compiler_params=pltpu.CompilerParams(vmem_limit_bytes=VMEM),
        cost_estimate=pl.CostEstimate(flops=terms * 6 * R * R * F, bytes_accessed=terms * R * F * 8, transcendentals=0),
        name="contributions",
    )(par, *mats, *units, proj)


PLAN_OUT = (
    ((N, ((1, 0, M), (1, 1, E), (1, 2, O), (1, 3, X))), (E, ((0, 1, N),)), (M, ((0, 0, N),))),
    ((N, ((1, 0, M), (1, 1, X), (1, 2, O))), (E, ()), (M, ((0, 0, N),))),
)
PLAN_IN = (
    ((X, ((0, 3, N),)), (O, ((0, 2, N), (0, 4, O)))),
    ((X, ((0, 1, N), (0, 3, O))), (O, ((0, 2, N), (1, 3, X), (0, 4, O)))),
)


def per_device(embeddings, partner):
    blk = lax.axis_index("blk")
    count = lax.axis_size("blk")
    par1 = (blk % 2).astype(jnp.int32)
    par = par1.reshape(1)
    even = par1 == 0

    def shift(v, steps):
        return lax.ppermute(v, "blk", [(i, (i + steps) % count) for i in range(count)])

    def cores(v):
        return lax.ppermute(v, "blk", [(i, i ^ 1) for i in range(count)])

    def feats(v):
        return lax.ppermute(v, "feat", [(0, 1), (1, 0)])

    own = embeddings
    right = shift(own, -2)
    left = shift(own, 2)
    other = cores(own)

    ss = jnp.sum(own * own, axis=1)
    inv = 1.0 / jnp.sqrt(ss + feats(ss) + 1e-06)
    pack = jnp.stack([inv, partner.astype(F32)])
    pack_x = cores(pack)
    node = jnp.where(even, jnp.stack([pack, pack_x]), jnp.stack([pack_x, pack]))
    node_l, node_r = shift(node, 2), shift(node, -2)
    far_l, far_r = shift(node[:, 1], 4), shift(node[:, 1], -4)
    near = jnp.concatenate([far_l, node_l[:, 1], node[:, 1], node_r[:, 1], far_r], axis=0).reshape(-1, 1)
    row_ids = blk * R + jnp.arange(R, dtype=jnp.int32)
    counts = 1.0 + jnp.sum((near == row_ids.astype(F32)[None, :]).astype(F32), axis=0)

    def vectors(cells):
        v = jnp.stack(cells)
        return jnp.pad(v, ((0, 0), (0, 8 - v.shape[1]), (0, 0)))

    mine = lambda v: jnp.where(even, v[0], v[1])
    packs = [mine(node_l), node_l[1], pack, pack_x, mine(node_r)]
    vec = vectors(packs)
    ids = (
        jnp.stack([blk + count - 2, blk + count - 1, blk, blk + 1 - 2 * par1, blk + 2]) % count * R
    ).astype(jnp.int32)

    near_scores = partial_scores(par, {O: own, X: other}, own, ((O,), (O, X)))
    extra = lax.ppermute(left, "blk", [(i + 1, i) for i in range(0, count, 2)])
    far_scores = partial_scores(
        par, {M: left, E: extra, O: own, X: other}, right, ((M, E, O, X), (M, X, O))
    )
    near_got = feats(near_scores)
    far_got = feats(far_scores)

    def slots(near, far):
        return jnp.concatenate([far[0:3], jnp.where(even, far[3:4], near[1:2]), near[0:1]], axis=0)

    units = split_units([left, extra, own, other, right], vec)
    scores, sums = score_sums(par, slots(near_scores, far_scores), slots(near_got, far_got), vec)
    sums = sums[:, 0]

    def home(v):
        to_prev = [(i, (i - 1) % count) for i in range(0, count, 2)]
        return v[O] + cores(v[X]) + shift(v[N], 2) + shift(v[M], -2) + lax.ppermute(v[E], "blk", to_prev)

    total = home(sums)
    lse = 10.0 + jnp.log(total)
    a = counts * 0.5 / total
    from_prev = [((i - 1) % count, i) for i in range(0, count, 2)]
    a_all = [shift(a, 2), lax.ppermute(a, "blk", from_prev), a, cores(a), shift(a, -2)]
    vec2 = vectors([jnp.concatenate([p, q[None]], axis=0) for p, q in zip(packs, a_all)])

    ch, cl, th, tl, proj, spos = coefficients(par, scores, vec2, ids)
    mats = (ch, cl, th, tl)
    to_right, to_prev, to_left = contributions(par, mats, units, proj, PLAN_OUT)
    got_next = lax.ppermute(to_prev, "blk", [(i, (i - 1) % count) for i in range(0, count, 2)])
    to_other, kept = contributions(par, mats, units, proj, PLAN_IN)
    from_left = shift(to_right, 2)
    from_right = shift(to_left, -2)
    from_other = cores(to_other)

    loss = jnp.sum(counts * lse) * 0.5 - jnp.sum(spos)
    step = 1
    while step < count:
        loss = loss + lax.ppermute(loss, "blk", [(i, i ^ step) for i in range(count)])
        step *= 2
    loss = loss / (count * R)

    grad = kept + from_left + from_right + from_other + got_next
    along = grad[R, 0:R]
    grads = (grad[0:R] * 10.0 - own * (inv * along)[:, None]) * inv[:, None]
    return (loss, grads)


def solution(mesh):
    in_specs = (P("blk", "feat"), P("blk"))
    out_specs = (P(), P("blk", "feat"))
    return jax.shard_map(per_device, mesh=mesh, in_specs=in_specs, out_specs=out_specs, check_vma=False)
```

time: 895 us -> 446 us (0.50)
  blocking collectives: 262 us -> 0 us
  other arithmetic: 189 us -> 19.9 us
  Pallas kernels: 0 us -> 90.8 us
  matrix products: 74.5 us -> 0 us
  local copies, waits for them, and re-layouts: 59.5 us -> 7.03 us
  waiting for transfers between devices: 184 us -> 219 us
  between operations: 16.4 us -> 7.19 us
    scatter-add x1 -> x0, other arithmetic: 175 us -> none  [per_device(): jax.ops.segment_sum(jnp.ones((total_rows,), jnp.float32), table, num_segm...]
    psum x3 -> x0, blocking collectives: 174 us -> none  [the longest x1 164 us: per_device(): loss = lax.psum(loss_local, 'blk') / total_rows]
    pallas_call x0 -> x7, Pallas kernels: none -> 90.8 us  [the longest x2 32.4 us: partial_scores(): pl.pallas_call(functools.partial(scores_kernel, lefts), out_shape=jax.Sha...]
    all_gather x1 -> x0, blocking collectives: 88.6 us -> none  [per_device(): table = lax.all_gather(partner, 'blk', axis=0, tiled=True)]
    dot_general x2 -> x0, matrix products: 74.5 us -> none  [the longest x1 42.2 us: sharpened_right_similarities(): jnp.dot(left, right, precision=lax.Precision.HIGHEST, preferred_element_t...]
    gather x3 -> x0, local copies, waits for them, and re-layouts: 51.3 us -> none  [the longest x1 24.1 us: per_device(): counts_all[col_ids]]
    ppermute x16 -> x30, waiting for transfers between devices: 184 us -> 219 us  [the longest x3 84.2 us: feats(): return lax.ppermute(v, 'feat', [(0, 1), (1, 0)])]
    ppermute x16 -> x30, starting transfers between devices: 108 us -> 101 us  [the longest x12 43.5 us: shift(): lax.ppermute(v, 'blk', [(i, (i + steps) % count) for i in range(count)])]
  transfers between devices with their start and end apart: 17 -> 30, of which waited for: 5 -> 14; matrix products, arithmetic and copies ran while one was open for 25% -> 3% of each run, Pallas kernels for 0% -> 4%
where the time goes in v1:
time: 446 us; the launch traced here: 445 us
  waiting for transfers between devices  219 us (49%)
  starting transfers between devices  101 us (23%)
  Pallas kernels  90.8 us (20%)
  other arithmetic  19.9 us (4%)
  between operations  7.19 us (2%)
  local copies, waits for them, and re-layouts  7.03 us (2%)
    ppermute x3, waiting for transfers between devices, feats(): return lax.ppermute(v, 'feat', [(0, 1), (1, 0)])  84.2 us
    ppermute x12, waiting for transfers between devices, shift(): lax.ppermute(v, 'blk', [(i, (i + steps) % count) for i in range(count)])  81.4 us
    ppermute x12, starting transfers between devices, shift(): lax.ppermute(v, 'blk', [(i, (i + steps) % count) for i in range(count)])  43.5 us
    ppermute x6, starting transfers between devices, per_device(): lax.ppermute(loss, 'blk', [(i, i ^ step) for i in range(count)])  38.8 us
    ppermute x6, waiting for transfers between devices, per_device(): lax.ppermute(loss, 'blk', [(i, i ^ step) for i in range(count)])  38.5 us
    pallas_call x2, Pallas kernels, partial_scores(): pl.pallas_call(functools.partial(scores_kernel, lefts), out_shape=jax.Sha...  32.4 us
    pallas_call x2, Pallas kernels, contributions(): pl.pallas_call(functools.partial(contrib_kernel, plans), grid=(F // T,),...  29.9 us
    pallas_call x1, Pallas kernels, split_units(): pl.pallas_call(units_kernel, grid=(F // 256,), out_shape=(shape, shape),...  10.1 us
  transfers between devices with their start and end apart: 30, of which 14 were waited for; matrix products, arithmetic and copies ran while one was open for 3% of the time, Pallas kernels for 4%

profile of v1, /device:TPU:0, one launch (start us, length us, event | category | flops | bytes accessed | tf_op | source)
XLA Modules:
  0.0 445.1 jit_solution(4881087679420556834)
XLA Ops:
  0.6 1.7 collective-permute-start.6
  2.4 7.5 %collective-permute-start.9 = (f32[512,1024]{1,0:T(8,128)}, f32[512,1024]{1,0:T(8,128)}, u32[]{:S(2)}, u32[]{:S(2)}) collective-permute-start(f32[512,1024]{1,0:T(8,128)} %o.1), channel_id=1, source_target_pairs={{0,124},{2,126},{4,0},{6,2},{8,4},{10,6},{12,8},{14,10},{16,12},{1... | collective-permute-start | bytes 6291464 | tf_op jit(solution)/shard_map/ppermute | solution.py:300
  9.8 45.8 %collective-permute-done.6.refs_0_.m = f32[512,1024]{1,0:T(8,128)S(1)} collective-permute-done((f32[512,1024]{1,0:T(8,128)}, f32[512,1024]{1,0:T(8,128)S(1)}, u32[]{:S(2)}, u32[]{:S(2)}) %collective-permute-start.6) | collective-permute-done | bytes 2097184 | tf_op jit(solution)/shard_map/ppermute | solution.py:300
  55.6 1.3 collective-permute-start.7
  56.9 4.9 %collective-permute-done.7.refs_1_.e = f32[512,1024]{1,0:T(8,128)} collective-permute-done((f32[512,1024]{1,0:T(8,128)S(1)}, f32[512,1024]{1,0:T(8,128)}, u32[]{:S(2)}, u32[]{:S(2)}) %collective-permute-start.7) | collective-permute-done | bytes 2097184 | tf_op jit(solution)/shard_map/ppermute | solution.py:336
  61.8 24.2 %partial_scores.2 = f32[4,512,512]{2,1,0:T(8,128)} custom-call(s32[1]{0:T(128)} %bitcast.6.par_ref, f32[512,1024]{1,0:T(8,128)} %copy-done.3, f32[512,1024]{1,0:T(8,128)} %collective-permute-done.7.refs_1_.e, f32[512,1024]{1,0:T(8,128)} %o.1, f32[512,1024]{1,0:T(8,128)} %collective-permute-done.8.refs_3_.refs_1_.x, f32[512,1024]{1,0:T(8,128)} %collective-permute-done.9.refs_4_.n), custom_call_target="tpu_custom_call" | custom-call | flops 6442450944 | bytes 10485760 | tf_op jit(solution)/shard_map/partial_scores/pallas_call | solution.py:88
  86.8 1.5 collective-permute-start
  89.0 84.2 %collective-permute-done = f32[512]{0:T(512)S(1)} collective-permute-done((f32[512]{0:T(512)S(1)}, f32[512]{0:T(512)S(1)}, u32[]{:S(2)}, u32[]{:S(2)}) %collective-permute-start) | collective-permute-done | bytes 2080 | tf_op jit(solution)/shard_map/ppermute | solution.py:306
  173.3 1.1 collective-permute-done.1
  174.6 8.2 %partial_scores.3 = f32[2,512,512]{2,1,0:T(8,128)} custom-call(s32[1]{0:T(128)} %bitcast.6.par_ref, f32[512,1024]{1,0:T(8,128)} %o.1, f32[512,1024]{1,0:T(8,128)} %collective-permute-done.8.refs_3_.refs_1_.x, f32[512,1024]{1,0:T(8,128)} %o.1), custom_call_target="tpu_custom_call" | custom-call | flops 3221225472 | bytes 6291456 | tf_op jit(solution)/shard_map/partial_scores/pallas_call | solution.py:88
  183.4 3.8 collective-permute-start.5
  187.2 12.6 %collective-permute-start.4 = (f32[2,2,512]{2,1,0:T(2,128)S(1)}, f32[2,2,512]{2,1,0:T(2,128)S(1)}, u32[]{:S(2)}, u32[]{:S(2)}) collective-permute-start(f32[2,2,512]{2,1,0:T(2,128)S(1)} %maximum_select_fusion), channel_id=1, source_target_pairs={{0,124},{2,126},{4,0},{6,2},{8,4},{10,6},{12,8},{14,10},{16,12},{1... | collective-permute-start | bytes 24584 | tf_op jit(solution)/shard_map/ppermute | solution.py:300
  199.8 25.8 %collective-permute-done.4 = f32[2,2,512]{2,1,0:T(2,128)S(1)} collective-permute-done((f32[2,2,512]{2,1,0:T(2,128)S(1)}, f32[2,2,512]{2,1,0:T(2,128)S(1)}, u32[]{:S(2)}, u32[]{:S(2)}) %collective-permute-start.4) | collective-permute-done | bytes 8224 | tf_op jit(solution)/shard_map/ppermute | solution.py:300
  225.6 4.3 collective-permute-done.2
  230.7 2.3 slice.105
  233.3 1.6 slice_select_fusion.1
  234.8 2.9 pad_maximum_fusion.mine
  237.8 2.2 slice.109
  240.0 1.6 slice_select_fusion
  241.5 3.0 pad_maximum_fusion.1.theirs
  244.5 8.5 %score_sums.1 = (f32[5,512,512]{2,1,0:T(8,128)}, f32[5,8,512]{2,1,0:T(8,128)}) custom-call(s32[1]{0:T(128)} %bitcast.6.par_ref, f32[5,512,512]{2,1,0:T(8,128)} %pad_maximum_fusion.mine, f32[5,512,512]{2,1,0:T(8,128)} %pad_maximum_fusion.1.theirs, f32[5,8,512]{2,1,0:T(8,128)} %pad.8.vec), custom_call_target="tpu_custom_call" | custom-call | tf_op jit(solution)/shard_map/score_sums/pallas_call | solution.py:142
  253.0 0.8 fusion.6
  253.8 9.8 %collective-permute-start.15 = (f32[512]{0:T(512)S(1)}, f32[512]{0:T(512)S(1)}, u32[]{:S(2)}, u32[]{:S(2)}) collective-permute-start(f32[512]{0:T(512)S(1)} %bitcast.76), channel_id=1, source_target_pairs={{0,126},{4,2},{8,6},{12,10},{16,14},{20,18},{24,22},{28,26},{32,30... | collective-permute-start | bytes 6152 | tf_op jit(solution)/shard_map/ppermute | solution.py:352
  264.2 1.6 collective-permute-start.13
  265.8 2.3 convert_reduce_fusion
  268.0 5.5 %collective-permute-done.13 = f32[512]{0:T(512)S(1)} collective-permute-done((f32[512]{0:T(512)S(1)}, f32[512]{0:T(512)S(1)}, u32[]{:S(2)}, u32[]{:S(2)}) %collective-permute-start.13) | collective-permute-done | bytes 2080 | tf_op jit(solution)/shard_map/ppermute | solution.py:300
  273.8 10.1 %split_units.1 = (bf16[5,512,1024]{2,1,0:T(8,128)(2,1)}, bf16[5,512,1024]{2,1,0:T(8,128)(2,1)}) custom-call(f32[512,1024]{1,0:T(8,128)} %copy-done.3, f32[512,1024]{1,0:T(8,128)} %collective-permute-done.7.refs_1_.e, f32[512,1024]{1,0:T(8,128)} %o.1, f32[512,1024]{1,0:T(8,128)} %collective-permute-done.8.refs_3_.refs_1_.x, ...), custom_call_target="tpu_custom_call" | custom-call | tf_op jit(solution)/shard_map/split_units/pallas_call | solution.py:232
  283.9 7.7 %collective-permute-start.19 = (f32[512]{0:T(512)S(1)}, f32[512]{0:T(512)S(1)}, u32[]{:S(2)}, u32[]{:S(2)}) collective-permute-start(f32[512]{0:T(512)S(1)} %get-tuple-element.32), channel_id=1, source_target_pairs={{0,124},{2,126},{4,0},{6,2},{8,4},{10,6},{12,8},{14,10},{16,12},{1... | collective-permute-start | bytes 6152 | tf_op jit(solution)/shard_map/ppermute | solution.py:300
  291.6 1.3 collective-permute-start.17
  292.9 9.3 %collective-permute-done.17 = f32[512]{0:T(512)S(1)} collective-permute-done((f32[512]{0:T(512)S(1)}, f32[512]{0:T(512)S(1)}, u32[]{:S(2)}, u32[]{:S(2)}) %collective-permute-start.17) | collective-permute-done | bytes 2080 | tf_op jit(solution)/shard_map/ppermute | solution.py:358
  303.0 10.0 %coefficients.1 = (bf16[5,512,512]{2,1,0:T(8,128)(2,1)}, bf16[5,512,512]{2,1,0:T(8,128)(2,1)}, bf16[5,512,512]{2,1,0:T(8,128)(2,1)}, bf16[5,512,512]{2,1,0:T(8,1...) custom-call(s32[1]{0:T(128)} %bitcast.6.par_ref, f32[5,512,512]{2,1,0:T(8,128)} %get-tuple-element.18.sc_ref, ...), custom_call_target="tpu_custom_call" | custom-call | tf_op jit(solution)/shard_map/coefficients/pallas_call | solution.py:203
  313.0 12.3 %contributions.2 = (f32[520,1024]{1,0:T(8,128)}, f32[520,1024]{1,0:T(8,128)}) custom-call(s32[1]{0:T(128)} %bitcast.6.par_ref, bf16[5,512,512]{2,1,0:T(8,128)(2,1)} %get-tuple-element.20.ch, bf16[5,512,512]{2,1,0:T(8,128)(2,1)} %get-tuple-element.21.cl, bf16[5,512,512]{2,1,0:T(8,128)(2,1)} %get-tuple-element.22.th, ...), custom_call_target="tpu_custom_call" | custom-call | flops 4831838208 | bytes 12582912 | tf_op jit(solution)/shard_map/contributions/pallas_call | solution.py:270
  325.3 17.6 %contributions.3 = (f32[520,1024]{1,0:T(8,128)}, f32[520,1024]{1,0:T(8,128)}, f32[520,1024]{1,0:T(8,128)}) custom-call(s32[1]{0:T(128)} %bitcast.6.par_ref, bf16[5,512,512]{2,1,0:T(8,128)(2,1)} %get-tuple-element.20.ch, bf16[5,512,512]{2,1,0:T(8,128)(2,1)} %get-tuple-element.21.cl, bf16[5,512,512]{2,1,0:T(8,128)(2,1)} %get-tuple-element.22.th, ...), custom_call_target="tpu_custom_call" | custom-call | flops 9663676416 | bytes 25165824 | tf_op jit(solution)/shard_map/contributions/pallas_call | solution.py:270
  342.9 7.7 %collective-permute-start.27 = (f32[520,1024]{1,0:T(8,128)}, f32[520,1024]{1,0:T(8,128)}, u32[]{:S(2)}, u32[]{:S(2)}) collective-permute-start(f32[520,1024]{1,0:T(8,128)} %get-tuple-element.29), channel_id=1, source_target_pairs={{0,124},{2,126},{4,0},{6,2},{8,4},{10,6},{12,8},{14,10},{16,12},{1... | collective-permute-start | bytes 6389768 | tf_op jit(solution)/shard_map/ppermute | solution.py:300
  350.7 3.0 collective-permute-start.29
  356.2 1.0 collective-permute-start.20
  358.2 31.5 %collective-permute-start.21 = (f32[]{:T(128)}, f32[]{:T(128)}, u32[]{:S(2)}, u32[]{:S(2)}) collective-permute-start(f32[]{:T(128)} %add.114), channel_id=1, source_target_pairs={{0,4},{2,6},{4,0},{6,2},{8,12},{10,14},{12,8},{14,10},{16,20},{18,... | collective-permute-start | bytes 20 | tf_op jit(solution)/shard_map/ppermute | solution.py:373
  389.7 25.0 %collective-permute-done.21 = f32[]{:T(128)} collective-permute-done((f32[]{:T(128)}, f32[]{:T(128)}, u32[]{:S(2)}, u32[]{:S(2)}) %collective-permute-start.21) | collective-permute-done | bytes 36 | tf_op jit(solution)/shard_map/ppermute | solution.py:373
  415.4 1.4 collective-permute-start.22
  416.7 3.8 collective-permute-done.22
  421.2 1.4 collective-permute-start.23
  422.6 3.8 collective-permute-done.23
  427.1 1.4 collective-permute-start.24
  428.5 2.3 collective-permute-done.24
  431.4 2.1 collective-permute-start.25
  433.5 3.1 collective-permute-done.25
  437.3 4.9 %add_add_fusion = f32[520,1024]{1,0:T(8,128)S(1)} fusion(f32[520,1024]{1,0:T(8,128)} %collective-permute-done.29, f32[520,1024]{1,0:T(8,128)} %collective-permute-done.28, f32[520,1024]{1,0:T(8,128)} %collective-permute-done.27, f32[520,1024]{1,0:T(8,128)S(1)} %copy-done.2, f32[520,1024]{1,0:T(8,128)} %collective-permute-done.26), kind=kLoop, calls=%fused_computation.3 | loop fusion | flops 2129920 | bytes 12779520 | tf_op jit(solution)/shard_map/add | solution.py:377
  442.3 1.7 fusion.1
  (77 shorter events, 6.6 us)
Async XLA Ops:
  0.6 54.9 %collective-permute-start.6 = (f32[512,1024]{1,0:T(8,128)}, f32[512,1024]{1,0:T(8,128)S(1)}, u32[]{:S(2)}, u32[]{:S(2)}) collective-permute-start(f32[512,1024]{1,0:T(8,128)} %o.1), channel_id=1, source_target_pairs={{0,4},{2,6},{4,8},{6,10},{8,12},{10,14},{12,16},{14,18},{16,20},{1... | collective-permute-start | bytes 6291464 | tf_op jit(solution)/shard_map/ppermute | solution.py:300
  2.4 54.5 %collective-permute-start.9 = (f32[512,1024]{1,0:T(8,128)}, f32[512,1024]{1,0:T(8,128)}, u32[]{:S(2)}, u32[]{:S(2)}) collective-permute-start(f32[512,1024]{1,0:T(8,128)} %o.1), channel_id=1, source_target_pairs={{0,124},{2,126},{4,0},{6,2},{8,4},{10,6},{12,8},{14,10},{16,12},{1... | collective-permute-start | bytes 6291464 | tf_op jit(solution)/shard_map/ppermute | solution.py:300
  9.8 47.1 %collective-permute-start.8 = (f32[512,1024]{1,0:T(8,128)}, f32[512,1024]{1,0:T(8,128)}, u32[]{:S(2)}, u32[]{:S(2)}) collective-permute-start(f32[512,1024]{1,0:T(8,128)} %o.1), channel_id=1, source_target_pairs={{0,2},{2,0},{4,6},{6,4},{8,10},{10,8},{12,14},{14,12},{16,18},{18,... | collective-permute-start | bytes 6291464 | tf_op jit(solution)/shard_map/ppermute | solution.py:303
  55.6 6.2 %copy-start.3 = (f32[512,1024]{1,0:T(8,128)}, f32[512,1024]{1,0:T(8,128)S(1)}, u32[]{:S(2)}) copy-start(f32[512,1024]{1,0:T(8,128)S(1)} %collective-permute-done.6.refs_0_.m) | copy-start | bytes 6291460
  55.6 6.2 %collective-permute-start.7 = (f32[512,1024]{1,0:T(8,128)S(1)}, f32[512,1024]{1,0:T(8,128)}, u32[]{:S(2)}, u32[]{:S(2)}) collective-permute-start(f32[512,1024]{1,0:T(8,128)S(1)} %collective-permute-done.6.refs_0_.m), channel_id=1, source_target_pairs={{2,0},{6,4},{10,8},{14,12},{18,16},{22,20},{26,24},{30,28},{34,32}... | collective-permute-start | bytes 6291464 | tf_op jit(solution)/shard_map/ppermute | solution.py:336
  61.8 24.9 %copy-start = (f32[512,1024]{1,0:T(8,128)S(1)}, f32[512,1024]{1,0:T(8,128)}, u32[]{:S(2)}) copy-start(f32[512,1024]{1,0:T(8,128)} %o.1) | copy-start | bytes 6291460
  61.8 27.2 %copy-start.6 = (s32[512]{0:T(512)S(1)}, s32[512]{0:T(512)}, u32[]{:S(2)}) copy-start(s32[512]{0:T(512)} %param.3) | copy-start | bytes 6148
  85.9 151.8 %collective-permute-start.10 = (f32[4,512,512]{2,1,0:T(8,128)}, f32[4,512,512]{2,1,0:T(8,128)}, u32[]{:S(2)}, u32[]{:S(2)}) collective-permute-start(f32[4,512,512]{2,1,0:T(8,128)} %partial_scores.2), channel_id=1, source_target_pairs={{0,1},{1,0},{2,3},{3,2},{4,5},{5,4},{6,7},{7,6},{8,9},{9,8},{10,11... | collective-permute-start | bytes 12582920 | tf_op jit(solution)/shard_map/ppermute | solution.py:306
  86.8 86.4 %collective-permute-start = (f32[512]{0:T(512)S(1)}, f32[512]{0:T(512)S(1)}, u32[]{:S(2)}, u32[]{:S(2)}) collective-permute-start(f32[512]{0:T(512)S(1)} %multiply_reduce_fusion), channel_id=1, source_target_pairs={{0,1},{1,0},{2,3},{3,2},{4,5},{5,4},{6,7},{7,6},{8,9},{9,8},{10,11... | collective-permute-start | bytes 6152 | tf_op jit(solution)/shard_map/ppermute | solution.py:306
  173.2 1.2 collective-permute-start.1
  174.5 12.7 %collective-permute-start.3 = (f32[2,2,512]{2,0,1:T(2,128)S(1)}, f32[2,2,512]{2,0,1:T(2,128)S(1)}, u32[]{:S(2)}, u32[]{:S(2)}) collective-permute-start(f32[2,2,512]{2,0,1:T(2,128)S(1)} %copy.9), channel_id=1, source_target_pairs={{0,4},{2,6},{4,8},{6,10},{8,12},{10,14},{12,16},{14,18},{16,20},{1... | collective-permute-start | bytes 24584 | tf_op jit(solution)/shard_map/ppermute | solution.py:300
  182.7 57.2 %collective-permute-start.11 = (f32[2,512,512]{2,1,0:T(8,128)}, f32[2,512,512]{2,1,0:T(8,128)S(1)}, u32[]{:S(2)}, u32[]{:S(2)}) collective-permute-start(f32[2,512,512]{2,1,0:T(8,128)} %partial_scores.3), channel_id=1, source_target_pairs={{0,1},{1,0},{2,3},{3,2},{4,5},{5,4},{6,7},{7,6},{8,9},{9,8},{10,11... | collective-permute-start | bytes 6291464 | tf_op jit(solution)/shard_map/ppermute | solution.py:306
  183.4 42.2 %collective-permute-start.5 = (f32[2,512]{1,0:T(2,128)S(1)}, f32[2,512]{1,0:T(2,128)S(1)}, u32[]{:S(2)}, u32[]{:S(2)}) collective-permute-start(f32[2,512]{1,0:T(2,128)S(1)} %slice_bitcast_fusion.1), channel_id=1, source_target_pairs={{0,120},{2,122},{4,124},{6,126},{8,0},{10,2},{12,4},{14,6},{16,8},... | collective-permute-start | bytes 12296 | tf_op jit(solution)/shard_map/ppermute | solution.py:300
  187.2 42.7 %collective-permute-start.2 = (f32[2,512]{1,0:T(2,128)S(1)}, f32[2,512]{1,0:T(2,128)S(1)}, u32[]{:S(2)}, u32[]{:S(2)}) collective-permute-start(f32[2,512]{1,0:T(2,128)S(1)} %slice_bitcast_fusion.1), channel_id=1, source_target_pairs={{0,8},{2,10},{4,12},{6,14},{8,16},{10,18},{12,20},{14,22},{16,24},... | collective-permute-start | bytes 12296 | tf_op jit(solution)/shard_map/ppermute | solution.py:300
  187.2 38.4 %collective-permute-start.4 = (f32[2,2,512]{2,1,0:T(2,128)S(1)}, f32[2,2,512]{2,1,0:T(2,128)S(1)}, u32[]{:S(2)}, u32[]{:S(2)}) collective-permute-start(f32[2,2,512]{2,1,0:T(2,128)S(1)} %maximum_select_fusion), channel_id=1, source_target_pairs={{0,124},{2,126},{4,0},{6,2},{8,4},{10,6},{12,8},{14,10},{16,12},{1... | collective-permute-start | bytes 24584 | tf_op jit(solution)/shard_map/ppermute | solution.py:300
  230.7 2.5 copy-start.4
  253.8 14.3 %collective-permute-start.15 = (f32[512]{0:T(512)S(1)}, f32[512]{0:T(512)S(1)}, u32[]{:S(2)}, u32[]{:S(2)}) collective-permute-start(f32[512]{0:T(512)S(1)} %bitcast.76), channel_id=1, source_target_pairs={{0,126},{4,2},{8,6},{12,10},{16,14},{20,18},{24,22},{28,26},{32,30... | collective-permute-start | bytes 6152 | tf_op jit(solution)/shard_map/ppermute | solution.py:352
  263.6 4.5 %collective-permute-start.12 = (f32[512]{0:T(512)S(1)}, f32[512]{0:T(512)S(1)}, u32[]{:S(2)}, u32[]{:S(2)}) collective-permute-start(f32[512]{0:T(512)S(1)} %bitcast.73), channel_id=1, source_target_pairs={{0,2},{2,0},{4,6},{6,4},{8,10},{10,8},{12,14},{14,12},{16,18},{18,... | collective-permute-start | bytes 6152 | tf_op jit(solution)/shard_map/ppermute | solution.py:303
  263.7 4.4 collective-permute-start.14
  264.2 9.3 %collective-permute-start.13 = (f32[512]{0:T(512)S(1)}, f32[512]{0:T(512)S(1)}, u32[]{:S(2)}, u32[]{:S(2)}) collective-permute-start(f32[512]{0:T(512)S(1)} %bitcast.71), channel_id=1, source_target_pairs={{0,4},{2,6},{4,8},{6,10},{8,12},{10,14},{12,16},{14,18},{16,20},{1... | collective-permute-start | bytes 6152 | tf_op jit(solution)/shard_map/ppermute | solution.py:300
  273.5 19.4 %collective-permute-start.16 = (f32[512]{0:T(512)S(1)}, f32[512]{0:T(512)S(1)}, u32[]{:S(2)}, u32[]{:S(2)}) collective-permute-start(f32[512]{0:T(512)S(1)} %get-tuple-element.32), channel_id=1, source_target_pairs={{0,4},{2,6},{4,8},{6,10},{8,12},{10,14},{12,16},{14,18},{16,20},{1... | collective-permute-start | bytes 6152 | tf_op jit(solution)/shard_map/ppermute | solution.py:300
  283.9 18.4 %collective-permute-start.19 = (f32[512]{0:T(512)S(1)}, f32[512]{0:T(512)S(1)}, u32[]{:S(2)}, u32[]{:S(2)}) collective-permute-start(f32[512]{0:T(512)S(1)} %get-tuple-element.32), channel_id=1, source_target_pairs={{0,124},{2,126},{4,0},{6,2},{8,4},{10,6},{12,8},{14,10},{16,12},{1... | collective-permute-start | bytes 6152 | tf_op jit(solution)/shard_map/ppermute | solution.py:300
  291.6 10.7 %collective-permute-start.18 = (f32[512]{0:T(512)S(1)}, f32[512]{0:T(512)S(1)}, u32[]{:S(2)}, u32[]{:S(2)}) collective-permute-start(f32[512]{0:T(512)S(1)} %get-tuple-element.32), channel_id=1, source_target_pairs={{0,2},{2,0},{4,6},{6,4},{8,10},{10,8},{12,14},{14,12},{16,18},{18,... | collective-permute-start | bytes 6152 | tf_op jit(solution)/shard_map/ppermute | solution.py:303
  291.6 10.6 %collective-permute-start.17 = (f32[512]{0:T(512)S(1)}, f32[512]{0:T(512)S(1)}, u32[]{:S(2)}, u32[]{:S(2)}) collective-permute-start(f32[512]{0:T(512)S(1)} %get-tuple-element.32), channel_id=1, source_target_pairs={{126,0},{2,4},{6,8},{10,12},{14,16},{18,20},{22,24},{26,28},{30,32... | collective-permute-start | bytes 6152 | tf_op jit(solution)/shard_map/ppermute | solution.py:358
  325.3 29.7 %copy-start.5 = (f32[8,512]{1,0:T(8,128)S(1)}, f32[8,512]{1,0:T(8,128)}, u32[]{:S(2)}) copy-start(f32[8,512]{1,0:T(8,128)} %get-tuple-element.19) | copy-start | bytes 49156
  325.3 112.0 %copy-start.2 = (f32[520,1024]{1,0:T(8,128)S(1)}, f32[520,1024]{1,0:T(8,128)}, u32[]{:S(2)}) copy-start(f32[520,1024]{1,0:T(8,128)} %get-tuple-element.27) | copy-start | bytes 6389764
  342.9 94.4 %collective-permute-start.28 = (f32[520,1024]{1,0:T(8,128)}, f32[520,1024]{1,0:T(8,128)}, u32[]{:S(2)}, u32[]{:S(2)}) collective-permute-start(f32[520,1024]{1,0:T(8,128)} %get-tuple-element.30), channel_id=1, source_target_pairs={{0,2},{2,0},{4,6},{6,4},{8,10},{10,8},{12,14},{14,12},{16,18},{18,... | collective-permute-start | bytes 6389768 | tf_op jit(solution)/shard_map/ppermute | solution.py:303
  342.9 94.4 %collective-permute-start.26 = (f32[520,1024]{1,0:T(8,128)}, f32[520,1024]{1,0:T(8,128)}, u32[]{:S(2)}, u32[]{:S(2)}) collective-permute-start(f32[520,1024]{1,0:T(8,128)} %get-tuple-element.28), channel_id=1, source_target_pairs={{0,4},{2,6},{4,8},{6,10},{8,12},{10,14},{12,16},{14,18},{16,20},{1... | collective-permute-start | bytes 6389768 | tf_op jit(solution)/shard_map/ppermute | solution.py:300
  342.9 94.4 %collective-permute-start.27 = (f32[520,1024]{1,0:T(8,128)}, f32[520,1024]{1,0:T(8,128)}, u32[]{:S(2)}, u32[]{:S(2)}) collective-permute-start(f32[520,1024]{1,0:T(8,128)} %get-tuple-element.29), channel_id=1, source_target_pairs={{0,124},{2,126},{4,0},{6,2},{8,4},{10,6},{12,8},{14,10},{16,12},{1... | collective-permute-start | bytes 6389768 | tf_op jit(solution)/shard_map/ppermute | solution.py:300
  350.7 86.6 %collective-permute-start.29 = (f32[520,1024]{1,0:T(8,128)}, f32[520,1024]{1,0:T(8,128)}, u32[]{:S(2)}, u32[]{:S(2)}) collective-permute-start(f32[520,1024]{1,0:T(8,128)} %get-tuple-element.31), channel_id=1, source_target_pairs={{0,126},{4,2},{8,6},{12,10},{16,14},{20,18},{24,22},{28,26},{32,30... | collective-permute-start | bytes 6389768 | tf_op jit(solution)/shard_map/ppermute | solution.py:364
  356.2 1.3 collective-permute-start.20
  358.2 56.5 %collective-permute-start.21 = (f32[]{:T(128)}, f32[]{:T(128)}, u32[]{:S(2)}, u32[]{:S(2)}) collective-permute-start(f32[]{:T(128)} %add.114), channel_id=1, source_target_pairs={{0,4},{2,6},{4,0},{6,2},{8,12},{10,14},{12,8},{14,10},{16,20},{18,... | collective-permute-start | bytes 20 | tf_op jit(solution)/shard_map/ppermute | solution.py:373
  415.4 5.2 %collective-permute-start.22 = (f32[]{:T(128)}, f32[]{:T(128)}, u32[]{:S(2)}, u32[]{:S(2)}) collective-permute-start(f32[]{:T(128)} %add.115), channel_id=1, source_target_pairs={{0,8},{2,10},{4,12},{6,14},{8,0},{10,2},{12,4},{14,6},{16,24},{18,... | collective-permute-start | bytes 20 | tf_op jit(solution)/shard_map/ppermute | solution.py:373
  421.2 5.2 %collective-permute-start.23 = (f32[]{:T(128)}, f32[]{:T(128)}, u32[]{:S(2)}, u32[]{:S(2)}) collective-permute-start(f32[]{:T(128)} %add.116), channel_id=1, source_target_pairs={{0,16},{2,18},{4,20},{6,22},{8,24},{10,26},{12,28},{14,30},{16,0},... | collective-permute-start | bytes 20 | tf_op jit(solution)/shard_map/ppermute | solution.py:373
  427.1 3.7 collective-permute-start.24
  431.4 5.2 %collective-permute-start.25 = (f32[]{:T(128)}, f32[]{:T(128)}, u32[]{:S(2)}, u32[]{:S(2)}) collective-permute-start(f32[]{:T(128)} %add.118), channel_id=1, source_target_pairs={{0,64},{2,66},{4,68},{6,70},{8,72},{10,74},{12,76},{14,78},{16,80}... | collective-permute-start | bytes 20 | tf_op jit(solution)/shard_map/ppermute | solution.py:373
  437.3 4.9 %copy-start.1 = (f32[512,1024]{1,0:T(8,128)S(1)}, f32[512,1024]{1,0:T(8,128)}, u32[]{:S(2)}) copy-start(f32[512,1024]{1,0:T(8,128)} %o.1) | copy-start | bytes 6291460
